TPU v7x, 256 devices: a whole 4x4x8 slice. The times are simulated.
256 devices in a mesh: lon: 8 (over y, core), lat: 16 (over z_hi, x), lev: 2 (over z_lo).
Axes of the slice: x: 4, y: 4, z: 8 (z_hi: 4, z_lo: 2; z = z_hi * 2 + z_lo), core: 2. Of those that a mesh axis runs over, the one named last changes fastest.
Arguments:
- fields_grid: float32 [6, 2, 1024, 8192], P(None, 'lev', 'lat', 'lon'), may hold values from -6 to 6
- hermite_proj: float32 [1024, 1024], P('lat'), may hold values from -0.1875 to 0.1875
Outputs:
- spectrum: float32 [1024, 6, 2, 4096], P('lat', None, 'lev', 'lon')
All inputs are finite; a program needn't handle non-finite values.
Results may differ from a plain program's by a relative error of at most 0.00007.
Values sent between devices are 32-bit elements; how exact they have to be, the bound alone decides.
A program may use at most 128 MiB of HBM per device.

v0:
```python
import functools
import math

import jax
import jax.numpy as jnp
import ml_dtypes
import numpy as np
from jax import lax
from jax.experimental import pallas as pl
from jax.experimental.pallas import tpu as pltpu
from jax.sharding import PartitionSpec as P

MESH = pl.DeviceIdType.MESH
F32 = jnp.float32
BF16 = jnp.bfloat16
NLON = 8192
STEPS = 3


def split_np(table):
    high = table.astype(np.float32).astype(ml_dtypes.bfloat16)
    low = (table - high.astype(np.float64)).astype(np.float32).astype(ml_dtypes.bfloat16)
    return high, low


def tables():
    q = np.arange(64)
    p = np.arange(128)
    high_m = np.arange(32)
    first = 2.0 * np.pi * (np.outer(q, q) % 64) / 64
    first = np.concatenate([np.cos(first), -np.sin(first)], axis=0)
    f_high, f_low = split_np(first)
    first_cat = np.concatenate([f_high, f_low, f_high], axis=1)
    angle = 2.0 * np.pi * np.outer(q, p) / NLON
    twiddle = np.concatenate([np.cos(angle), np.sin(angle)], axis=0).astype(np.float32)
    second = 2.0 * np.pi * (np.outer(high_m, p) % 128) / 128
    cos_b, sin_b = np.cos(second), np.sin(second)
    second = np.concatenate(
        [np.concatenate([cos_b, sin_b], axis=1), np.concatenate([-sin_b, cos_b], axis=1)], axis=0
    ) / math.sqrt(NLON)
    s_high, s_low = split_np(second)
    second_cat = np.concatenate([s_high, s_low], axis=0)
    return first_cat, twiddle, second_cat


def split(value):
    high = value.astype(BF16)
    low = (value - high.astype(F32)).astype(BF16)
    return high, low


def wait_bytes(ref, sem):
    pltpu.make_async_copy(ref, ref, sem).wait()


def kernel(
    fields, herm, first_ref, twiddle_ref, second_ref, out_ref,
    halo, xs, xr, b_hi, b_lo, zs, zr, zct, pbuf, p_hi, p_lo, outs, gath,
    halo_send, halo_recv, lon_send, lon_recv, in_send, in_recv, out_send, out_recv,
    p_send, pz_recv, px_recv, pc_recv, round_two,
):
    lon = lax.axis_index("lon")
    lat = lax.axis_index("lat")
    lev = lax.axis_index("lev")
    yy, core = lon // 2, lax.rem(lon, 2)
    zz, xx = lat // 4, lax.rem(lat, 4)
    half, l8 = lax.rem(lat, 2), lat // 2
    other = 1 - lev

    own_rows = pl.ds(pl.multiple_of(lat * 64, 64), 64)
    for col in range(4):
        lanes = pl.ds(pl.multiple_of(core * 512 + col * 128, 128), 128)
        pltpu.make_async_copy(herm.at[:, lanes], pbuf.at[core, col, own_rows], pc_recv.at[1]).start()

    barrier = pltpu.get_barrier_semaphore()
    pl.semaphore_signal(barrier, inc=1, device_id=(lon, lat, other), device_id_type=MESH)
    for off in range(1, 8):
        pl.semaphore_signal(
            barrier, inc=1, device_id=(lax.rem(lon + off, 8), lat, lev), device_id_type=MESH
        )
    for off in range(1, 16):
        pl.semaphore_signal(
            barrier, inc=1, device_id=(lon, lax.rem(lat + off, 16), lev), device_id_type=MESH
        )
    pl.semaphore_wait(barrier, 23)

    halo_copies = []
    for slot, field in enumerate((2, 4)):
        copy = pltpu.make_async_remote_copy(
            src_ref=fields.at[field, 0], dst_ref=halo.at[slot],
            send_sem=halo_send.at[slot], recv_sem=halo_recv.at[slot],
            device_id=(lon, lat, other), device_id_type=MESH,
        )
        copy.start()
        halo_copies.append(copy)

    def make_products(dst_field, compute):
        @pl.loop(0, 8)
        def _(yb):
            rows = pl.ds(pl.multiple_of(yb * 8, 8), 8)
            value = compute(rows)
            for t in range(8):
                xs[pl.ds(dst_field * 512 + yb * 64 + t, 8, stride=8), :] = value[:, t * 128:(t + 1) * 128]

    def send_lon(step, to_core):
        field = 3 * to_core + step
        for dy in range(4):
            peer_y = lax.rem(yy + dy, 4)
            rows = pl.ds(pl.multiple_of(field * 512 + peer_y * 128, 128), 128)

            def remote():
                pltpu.make_async_remote_copy(
                    src_ref=xs.at[rows], dst_ref=xr.at[step, lon],
                    send_sem=lon_send.at[step], recv_sem=lon_recv.at[step],
                    device_id=(peer_y * 2 + to_core, lat, lev), device_id_type=MESH,
                ).start()

            if dy:
                remote()
            else:
                @pl.when(core != to_core)
                def _():
                    remote()

                @pl.when(core == to_core)
                def _():
                    pltpu.make_async_copy(xs.at[rows], xr.at[step, lon], lon_recv.at[step]).start()

    make_products(0, lambda r: fields[0, 0, r, :] * fields[5, 0, r, :])
    send_lon(0, 0)
    make_products(3, lambda r: fields[1, 0, r, :] * fields[3, 0, r, :])
    send_lon(0, 1)

    wait_bytes(herm.at[:, pl.ds(0, 512)], pc_recv.at[1])
    own = pbuf.at[core, :, own_rows]
    for dz in range(1, 4):
        pltpu.make_async_remote_copy(
            src_ref=own, dst_ref=own, send_sem=p_send.at[0], recv_sem=pz_recv.at[dz],
            device_id=(lon, lax.rem(zz + dz, 4) * 4 + xx, lev), device_id_type=MESH,
        ).start()
    for dx in range(1, 4):
        pltpu.make_async_remote_copy(
            src_ref=own, dst_ref=own, send_sem=p_send.at[1], recv_sem=px_recv.at[0, dx],
            device_id=(lon, zz * 4 + lax.rem(xx + dx, 4), lev), device_id_type=MESH,
        ).start()

    make_products(1, lambda r: fields[0, 0, r, :] * fields[1, 0, r, :])
    send_lon(1, 0)
    sign = jnp.where(lev == 0, F32(-0.5), F32(0.5))
    halo_copies[0].wait_recv()
    make_products(4, lambda r: halo[0, r, :] * (fields[0, 0, r, :] * sign))
    send_lon(1, 1)
    make_products(2, lambda r: fields[0, 0, r, :] * fields[4, 0, r, :])
    send_lon(2, 0)
    halo_copies[1].wait_recv()
    make_products(
        5,
        lambda r: halo[0, r, :] * (fields[3, 0, r, :] * sign)
        - 0.25 * (fields[4, 0, r, :] - 2.0 * halo[1, r, :]),
    )
    send_lon(2, 1)

    for dz in range(1, 4):
        wait_bytes(herm.at[:, pl.ds(0, 512)], pz_recv.at[dz])
        origin = lax.rem(zz + 4 - dz, 4) * 4 + xx
        rows = pl.ds(pl.multiple_of(origin * 64, 64), 64)
        for dx in range(1, 4):
            pltpu.make_async_remote_copy(
                src_ref=pbuf.at[core, :, rows], dst_ref=pbuf.at[core, :, rows],
                send_sem=p_send.at[1], recv_sem=px_recv.at[dz, dx],
                device_id=(lon, zz * 4 + lax.rem(xx + dx, 4), lev), device_id_type=MESH,
            ).start()

    def zonal(step):
        wait_bytes(xr.at[step], lon_recv.at[step])
        cos_t, sin_t = twiddle_ref[0:64, :], twiddle_ref[64:128, :]

        @pl.loop(0, 8)
        def _(u):
            cats = []
            for k in range(2):
                block = xr[step, :, pl.ds(pl.multiple_of(u * 16 + k * 8, 8), 8), :].reshape(64, 128)
                high, low = split(block)
                cats.append(jnp.concatenate([high, high, low], axis=0))
            cat = jnp.concatenate(cats, axis=1)
            first = jnp.dot(first_ref[...], cat, preferred_element_type=F32)
            res, ims = [], []
            for k in range(2):
                re = first[0:64, k * 128:(k + 1) * 128]
                im = first[64:128, k * 128:(k + 1) * 128]
                res.append((re * cos_t + im * sin_t).reshape(8, 8, 128))
                ims.append((im * cos_t - re * sin_t).reshape(8, 8, 128))
            rows = pl.ds(pl.multiple_of(u * 16, 16), 16)
            for part, pair in enumerate((res, ims)):
                high, low = split(jnp.concatenate(pair, axis=1))
                b_hi[:, rows, part * 128:(part + 1) * 128] = high
                b_lo[:, rows, part * 128:(part + 1) * 128] = low

        @pl.loop(0, 4)
        def _(u):
            pair = pl.ds(u * 2, 2)
            high = b_hi[pair].reshape(256, 256)
            low = b_lo[pair].reshape(256, 256)
            nt = (((1,), (1,)), ((), ()))
            one = lax.dot_general(second_ref[...], high, nt, preferred_element_type=F32)
            two = lax.dot_general(second_ref[0:64, :], low, nt, preferred_element_type=F32)
            both = one[0:64] + one[64:128] + two
            for k in range(2):
                zs[step, :, u * 2 + k] = both[:, k * 128:(k + 1) * 128].reshape(8, 8, 128)

    source = lat * 4 + yy
    my_g, my_s = source // 8, lax.rem(source, 8)

    def send_in(step):
        flip = jnp.logical_and(core == 1, step >= 1)
        to_lev = jnp.where(flip, other, lev)

        @pl.loop(0, 64)
        def _(j):
            dz, dx = j // 16, lax.rem(j // 8, 2)
            dy, dc = lax.rem(j // 2, 4), lax.rem(j, 2)
            to_x = lax.rem(xx + 2 * dx, 4) // 2 * 2 + core
            to_lat = lax.rem(zz + dz, 4) * 4 + to_x
            to_lon = lax.rem(yy + dy, 4) * 2 + lax.rem(core + dc, 2)
            mine = jnp.logical_and(jnp.logical_and(to_lat == lat, to_lon == lon), to_lev == lev)
            src = zs.at[step, to_lon, to_lat // 2]
            dst = zr.at[step, my_g, my_s]

            @pl.when(jnp.logical_not(mine))
            def _():
                pltpu.make_async_remote_copy(
                    src_ref=src, dst_ref=dst,
                    send_sem=in_send.at[step], recv_sem=in_recv.at[step],
                    device_id=(to_lon, to_lat, to_lev), device_id_type=MESH,
                ).start()

            @pl.when(mine)
            def _():
                pltpu.make_async_copy(src, dst, in_recv.at[step]).start()

    def wait_in_sends(step):
        flip = jnp.logical_and(core == 1, step >= 1)
        has_self = jnp.logical_and(half == core, jnp.logical_not(flip))

        @pl.when(has_self)
        def _():
            wait_bytes(zs.at[step, pl.ds(0, 7)], in_send.at[step])
            wait_bytes(zs.at[step, 0, pl.ds(0, 7)], in_send.at[step])

        @pl.when(jnp.logical_not(has_self))
        def _():
            wait_bytes(zs.at[step], in_send.at[step])

    zonal(0)
    for off in range(1, 16):
        pl.semaphore_signal(
            round_two, inc=1, device_id=(lon, lax.rem(lat + off, 16), lev), device_id_type=MESH
        )
    pl.semaphore_wait(round_two, 15)
    send_in(0)
    zonal(1)
    send_in(1)
    zonal(2)
    send_in(2)

    for dz in range(4):
        for dx in range(1, 4):
            wait_bytes(herm.at[:, pl.ds(0, 512)], px_recv.at[dz, dx])
    to_sibling = pltpu.make_async_remote_copy(
        src_ref=pbuf.at[core], dst_ref=pbuf.at[core],
        send_sem=p_send.at[2], recv_sem=pc_recv.at[0],
        device_id=(lon + 1 - 2 * core, lat, lev), device_id_type=MESH,
    )
    to_sibling.start()

    def prepare(which):
        @pl.loop(0, 64)
        def _(j):
            g, u = j // 8, lax.rem(j, 8)
            for col in range(4):
                pieces = [
                    pbuf[which, col, pl.ds(g * 128 + u * 2 + k, 8, stride=16), :]
                    for k in range(2)
                ]
                high, low = split(jnp.concatenate(pieces, axis=0))
                rows = pl.ds(pl.multiple_of(j * 16, 16), 16)
                p_hi[which, rows, col * 128:(col + 1) * 128] = high
                p_lo[which, rows, col * 128:(col + 1) * 128] = low

    prepare(core)
    wait_bytes(pbuf.at[0], pc_recv.at[0])
    prepare(1 - core)

    lane = lax.broadcasted_iota(jnp.int32, (64, 128), 1)

    def meridional(step):
        wait_bytes(zr.at[step], in_recv.at[step])
        v = [zr[step, :, s].reshape(64, 128) for s in range(8)]
        for k in range(3):
            bit = 1 << k
            low_half = (lane & bit) == 0
            new = list(v)
            for a in range(8):
                if a & bit:
                    continue
                b = a | bit
                new[a] = jnp.where(low_half, v[a], pltpu.roll(v[b], bit, 1))
                new[b] = jnp.where(low_half, pltpu.roll(v[a], 128 - bit, 1), v[b])
            v = new
        for j in range(8):
            for g in range(8):
                zct[g, pl.ds(j, 8, stride=8), :] = v[j][g * 8:(g + 1) * 8]
        high, low = split(jnp.concatenate([zct[g] for g in range(8)], axis=1))
        stacked = jnp.concatenate([high, low], axis=0)
        low_lanes = lax.broadcasted_iota(jnp.int32, (32, 128), 1) < 64
        for which in range(2):
            for col in range(2):
                cols = slice(col * 256, (col + 1) * 256)
                one = jnp.dot(stacked, p_hi[which, :, cols], preferred_element_type=F32)
                two = jnp.dot(high, p_lo[which, :, cols], preferred_element_type=F32)
                both = one[0:64] + one[64:128] + two
                for k in range(2):
                    t = which * 4 + col * 2 + k
                    a = both[0:32, k * 128:(k + 1) * 128]
                    b = both[32:64, k * 128:(k + 1) * 128]
                    even = jnp.where(low_lanes, a, pltpu.roll(b, 64, 1))
                    odd = jnp.where(low_lanes, pltpu.roll(a, 64, 1), b)
                    outs[step, 2 * t] = even.reshape(4, 8, 128)
                    outs[step, 2 * t + 1] = odd.reshape(4, 8, 128)

        pltpu.make_async_copy(
            outs.at[step, lat], gath.at[step, half, :, l8], out_recv.at[step]
        ).start()

        @pl.loop(1, 16)
        def _(j):
            to_lat = lax.rem(zz + j // 4, 4) * 4 + lax.rem(xx + lax.rem(j, 4), 4)
            pltpu.make_async_remote_copy(
                src_ref=outs.at[step, to_lat], dst_ref=gath.at[step, half, :, l8],
                send_sem=out_send.at[step], recv_sem=out_recv.at[step],
                device_id=(lon, to_lat, lev), device_id_type=MESH,
            ).start()

    for step in range(STEPS):
        meridional(step)

    def assemble(step):
        wait_bytes(gath.at[step], out_recv.at[step])
        for h2 in range(2):
            field = 3 * h2 + step
            for t in range(2):
                block = gath[step, h2, 2 * t:2 * t + 2].reshape(128, 128)
                turned = block.T
                for h in range(2):
                    sb = 2 * h + t
                    for n0 in range(0, 64, 8):
                        out_ref[pl.ds((n0 * 6 + field) * 4 + sb, 8, stride=24), :] = (
                            turned[h * 64 + n0:h * 64 + n0 + 8]
                        )

    for step in range(STEPS):
        assemble(step)

    for copy in halo_copies:
        copy.wait_send()
    for step in range(STEPS):
        wait_bytes(xs.at[pl.ds(0, 896)], lon_send.at[step])
        wait_in_sends(step)
        wait_bytes(outs.at[step, pl.ds(0, 15)], out_send.at[step])
    wait_bytes(pbuf.at[0, :, pl.ds(0, 192)], p_send.at[0])
    wait_bytes(pbuf.at[0, :, pl.ds(0, 768)], p_send.at[1])
    to_sibling.wait_send()


def on_device(fields_grid, hermite_proj):
    first_cat, twiddle, second_cat = tables()
    vmem = pl.BlockSpec(memory_space=pltpu.VMEM)
    dma = pltpu.SemaphoreType.DMA
    out = pl.pallas_call(
        kernel,
        out_shape=jax.ShapeDtypeStruct((1536, 128), F32),
        in_specs=[vmem] * 5,
        out_specs=vmem,
        scratch_shapes=[
            pltpu.VMEM((2, 64, 1024), F32),
            pltpu.VMEM((6 * 512, 128), F32),
            pltpu.VMEM((3, 8, 128, 128), F32),
            pltpu.VMEM((8, 128, 256), BF16),
            pltpu.VMEM((8, 128, 256), BF16),
            pltpu.VMEM((3, 8, 8, 8, 128), F32),
            pltpu.VMEM((3, 8, 8, 8, 128), F32),
            pltpu.VMEM((8, 64, 128), F32),
            pltpu.VMEM((2, 4, 1024, 128), F32),
            pltpu.VMEM((2, 1024, 512), BF16),
            pltpu.VMEM((2, 1024, 512), BF16),
            pltpu.VMEM((3, 16, 4, 8, 128), F32),
            pltpu.VMEM((3, 2, 4, 8, 8, 128), F32),
            dma((2,)), dma((2,)), dma((3,)), dma((3,)), dma((3,)), dma((3,)), dma((3,)), dma((3,)),
            dma((3,)), dma((4,)), dma((4, 4)), dma((2,)),
            pltpu.SemaphoreType.REGULAR,
        ],
        compiler_params=pltpu.CompilerParams(
            collective_id=0, has_side_effects=True, vmem_limit_bytes=48 * 1024 * 1024
        ),
    )(fields_grid, hermite_proj, first_cat, twiddle, second_cat)
    return out.reshape(64, 6, 1, 512)


def solution(mesh):
    in_specs = (P(None, "lev", "lat", "lon"), P("lat", None))
    out_specs = P("lat", None, "lev", "lon")
    return jax.shard_map(
        on_device, mesh=mesh, in_specs=in_specs, out_specs=out_specs, check_vma=False
    )
```

profile of v0, /device:TPU:1, one launch (start us, length us, event | category | flops | bytes accessed | tf_op | source)
XLA Modules:
  0.0 88.7 jit_solution(5881615099293801032)
XLA Ops:
  0.0 0.0 copy-start
  0.0 1.4 %copy-done = f32[6,1,64,1024]{3,2,1,0:T(8,128)S(1)} copy-done((f32[6,1,64,1024]{3,2,1,0:T(8,128)S(1)}, f32[6,1,64,1024]{3,2,1,0:T(8,128)}, u32[]{:S(2)}) %copy-start) | copy-done | bytes 1572888
  1.4 0.0 copy-start.1
  1.4 0.9 %copy-done.1 = f32[64,1024]{1,0:T(8,128)S(1)} copy-done((f32[64,1024]{1,0:T(8,128)S(1)}, f32[64,1024]{1,0:T(8,128)}, u32[]{:S(2)}) %copy-start.1) | copy-done | bytes 262168
  2.4 0.0 copy-start.2
  2.4 0.8 copy-done.2
  3.2 0.0 copy-start.3
  3.2 0.8 copy-done.3
  4.0 0.0 copy-start.4
  4.0 0.8 copy-done.4
  4.9 82.9 %shard_map.55 = f32[1536,128]{1,0:T(8,128)S(1)} custom-call(f32[6,1,64,1024]{3,2,1,0:T(8,128)S(1)} %copy-done, f32[64,1024]{1,0:T(8,128)S(1)} %copy-done.1, bf16[128,192]{1,0:T(8,128)(2,1)S(1)} %copy-done.4, f32[128,128]{1,0:T(8,128)S(1)} %copy-done.3, bf16[128,256]{1,0:T(8,128)(2,1)S(1)} %copy-done.2), custom_call_target="tpu_custom_call" | custom-call | tf_op jit(solution)/shard_map/pallas_call | solution.py:379
  87.8 0.9 copy.9
Async XLA Ops:
  0.0 1.4 %copy-start = (f32[6,1,64,1024]{3,2,1,0:T(8,128)S(1)}, f32[6,1,64,1024]{3,2,1,0:T(8,128)}, u32[]{:S(2)}) copy-start(f32[6,1,64,1024]{3,2,1,0:T(8,128)} %fields.1) | copy-start | bytes 4718596
  1.4 0.9 %copy-start.1 = (f32[64,1024]{1,0:T(8,128)S(1)}, f32[64,1024]{1,0:T(8,128)}, u32[]{:S(2)}) copy-start(f32[64,1024]{1,0:T(8,128)} %herm.1) | copy-start | bytes 786436
  2.4 0.8 copy-start.2
  3.2 0.8 copy-start.3
  4.0 0.8 copy-start.4
where the time goes:
time: 89 us; the launch traced here: 88.7 us
  Pallas kernels  82.9 us (93%)
  local copies, waits for them, and re-layouts  5.76 us (6%)
    pallas_call x1, Pallas kernels, on_device(): pl.pallas_call(kernel, out_shape=jax.ShapeDtypeStruct((1536, 128), F32),...  82.9 us
    unnamed x11, local copies, waits for them, and re-layouts  5.76 us

commit v1 on v0

v1 whole, which is shorter than its diff:
```python
import functools
import math

import jax
import jax.numpy as jnp
import ml_dtypes
import numpy as np
from jax import lax
from jax.experimental import pallas as pl
from jax.experimental.pallas import tpu as pltpu
from jax.sharding import PartitionSpec as P

MESH = pl.DeviceIdType.MESH
F32 = jnp.float32
BF16 = jnp.bfloat16
NLON = 8192
STEPS = 3


def split_np(table):
    high = table.astype(np.float32).astype(ml_dtypes.bfloat16)
    low = (table - high.astype(np.float64)).astype(np.float32).astype(ml_dtypes.bfloat16)
    return high, low


def tables():
    q = np.arange(64)
    p = np.arange(128)
    high_m = np.arange(32)
    first = 2.0 * np.pi * (np.outer(q, q) % 64) / 64
    first = np.concatenate([np.cos(first), -np.sin(first)], axis=0)
    f_high, f_low = split_np(first)
    first_cat = np.concatenate([f_high, f_low, f_high], axis=1)
    angle = 2.0 * np.pi * np.outer(q, p) / NLON
    twiddle = np.concatenate([np.cos(angle), np.sin(angle)], axis=0).astype(np.float32)
    second = 2.0 * np.pi * (np.outer(high_m, p) % 128) / 128
    cos_b, sin_b = np.cos(second), np.sin(second)
    second = np.concatenate(
        [np.concatenate([cos_b, sin_b], axis=1), np.concatenate([-sin_b, cos_b], axis=1)], axis=0
    ) / math.sqrt(NLON)
    s_high, s_low = split_np(second)
    second_cat = np.concatenate([s_high, s_low], axis=0)
    return first_cat, twiddle, second_cat


def split(value):
    high = value.astype(BF16)
    low = (value - high.astype(F32)).astype(BF16)
    return high, low


def wait_bytes(ref, sem):
    pltpu.make_async_copy(ref, ref, sem).wait()


def kernel(
    fields_hbm, herm_hbm, first_hbm, twiddle_hbm, second_hbm, out_ref,
    fields, first_ref, twiddle_ref, second_ref, halo, xs, xr, b_hi, b_lo, zs, zr, zct, pbuf, p_hi, p_lo, zb, outs, gath,
    halo_send, halo_recv, lon_send, lon_recv, in_send, in_recv, out_send, out_recv,
    p_send, pz_recv, px_recv, pc_recv, load, round_two,
):
    lon = lax.axis_index("lon")
    lat = lax.axis_index("lat")
    lev = lax.axis_index("lev")
    yy, core = lon // 2, lax.rem(lon, 2)
    zz, xx = lat // 4, lax.rem(lat, 4)
    half, l8 = lax.rem(lat, 2), lat // 2
    other = 1 - lev

    away = lax.rem(zz + 3 + 2 * lev, 4)
    partner_id = (lon, lat, other)
    away_id = (lon, away * 4 + xx, other)
    barrier = pltpu.get_barrier_semaphore()

    def greet(device_id):
        pl.semaphore_signal(barrier, inc=1, device_id=device_id, device_id_type=MESH)

    for off in range(1, 16):
        greet((lon, lax.rem(lat + off, 16), lev))
    greet(away_id)
    for off in range(1, 8):
        greet((lax.rem(lon + off, 8), lat, lev))
    for off in range(8):
        greet((lax.rem(lon + off, 8), lat, other))

    loads = [
        pltpu.make_async_copy(fields_hbm.at[f, 0], fields.at[f], load.at[f]) for f in (0, 5, 1, 3, 4)
    ]
    loads = dict(zip((0, 5, 1, 3, 4), loads))
    for copy in loads.values():
        copy.start()
    own_rows = pl.ds(pl.multiple_of(lat * 64, 64), 64)
    for col in range(4):
        lanes = pl.ds(pl.multiple_of(core * 512 + col * 128, 128), 128)
        pltpu.make_async_copy(herm_hbm.at[:, lanes], pbuf.at[core, col, own_rows], pc_recv.at[1]).start()
    constants = [
        pltpu.make_async_copy(hbm, ref, load.at[6 + n])
        for n, (hbm, ref) in enumerate(
            ((first_hbm, first_ref), (twiddle_hbm, twiddle_ref), (second_hbm, second_ref))
        )
    ]
    for copy in constants:
        copy.start()

    halo_copies = []
    for slot, field in enumerate((2, 4)):
        copy = pltpu.make_async_remote_copy(
            src_ref=fields_hbm.at[field, 0], dst_ref=halo.at[slot],
            send_sem=halo_send.at[slot], recv_sem=halo_recv.at[slot],
            device_id=partner_id, device_id_type=MESH,
        )
        halo_copies.append(copy)

    def make_products(dst_field, compute):
        @pl.loop(0, 8)
        def _(yb):
            rows = pl.ds(pl.multiple_of(yb * 8, 8), 8)
            value = compute(rows)
            for t in range(8):
                xs[pl.ds(dst_field * 512 + yb * 64 + t, 8, stride=8), :] = value[:, t * 128:(t + 1) * 128]

    def send_lon(step, to_core):
        field = 3 * to_core + step
        for dy in range(4):
            peer_y = lax.rem(yy + dy, 4)
            rows = pl.ds(pl.multiple_of(field * 512 + peer_y * 128, 128), 128)

            def remote():
                pltpu.make_async_remote_copy(
                    src_ref=xs.at[rows], dst_ref=xr.at[step, lon],
                    send_sem=lon_send.at[step], recv_sem=lon_recv.at[step],
                    device_id=(peer_y * 2 + to_core, lat, lev), device_id_type=MESH,
                ).start()

            if dy:
                remote()
            else:
                @pl.when(core != to_core)
                def _():
                    remote()

                @pl.when(core == to_core)
                def _():
                    pltpu.make_async_copy(xs.at[rows], xr.at[step, lon], lon_recv.at[step]).start()

    def wait_lon_sends(step):
        wait_bytes(xs.at[pl.ds(0, 896)], lon_send.at[step])

    beyond_id = (lon, away * 4 + xx, lev)
    quarter = pbuf.at[0, :, pl.ds(0, 64)]

    def rows_of(block_z, block_x, start=0, size=64):
        first = pl.multiple_of((block_z * 4 + block_x) * 64 + start, size)
        return pbuf.at[core, :, pl.ds(first, size)]

    def push(block, device_id, sem, slot):
        pltpu.make_async_remote_copy(
            src_ref=block, dst_ref=block, send_sem=p_send.at[slot], recv_sem=sem,
            device_id=device_id, device_id_type=MESH,
        ).start()

    right_id = (lon, zz * 4 + lax.rem(xx + 1, 4), lev)
    left_id = (lon, zz * 4 + lax.rem(xx + 3, 4), lev)

    def spread_x(slot, block_z):
        push(rows_of(block_z, xx), right_id, px_recv.at[slot, 0], 1)
        push(rows_of(block_z, xx), left_id, px_recv.at[slot, 1], 1)

    def relay_x(slot, block_z):
        left_x, right_x = lax.rem(xx + 3, 4), lax.rem(xx + 1, 4)
        wait_bytes(rows_of(block_z, left_x), px_recv.at[slot, 0])
        push(rows_of(block_z, left_x, 0, 32), right_id, px_recv.at[slot, 2], 3)
        wait_bytes(rows_of(block_z, right_x), px_recv.at[slot, 1])
        push(rows_of(block_z, right_x, 32, 32), left_id, px_recv.at[slot, 3], 3)

    toward = lax.rem(zz + 5 - 2 * lev, 4)
    far = lax.rem(zz + 2, 4)
    blocks = (zz, away, toward, far)

    def zonal(step):
        wait_bytes(xr.at[step], lon_recv.at[step])
        if step == 0:
            for copy in constants:
                copy.wait()
        cos_t, sin_t = twiddle_ref[0:64, :], twiddle_ref[64:128, :]

        for u in range(8):
            cats = []
            for k in range(2):
                block = xr[step, :, pl.ds(u * 16 + k * 8, 8), :].reshape(64, 128)
                high, low = split(block)
                cats.append(jnp.concatenate([high, high, low], axis=0))
            cat = jnp.concatenate(cats, axis=1)
            first = jnp.dot(first_ref[...], cat, preferred_element_type=F32)
            res, ims = [], []
            for k in range(2):
                re = first[0:64, k * 128:(k + 1) * 128]
                im = first[64:128, k * 128:(k + 1) * 128]
                res.append((re * cos_t + im * sin_t).reshape(8, 8, 128))
                ims.append((im * cos_t - re * sin_t).reshape(8, 8, 128))
            rows = pl.ds(u * 16, 16)
            for part, pair in enumerate((res, ims)):
                high, low = split(jnp.concatenate(pair, axis=1))
                b_hi[:, rows, part * 128:(part + 1) * 128] = high
                b_lo[:, rows, part * 128:(part + 1) * 128] = low

        for u in range(4):
            pair = pl.ds(u * 2, 2)
            high = b_hi[pair].reshape(256, 256)
            low = b_lo[pair].reshape(256, 256)
            nt = (((1,), (1,)), ((), ()))
            one = lax.dot_general(second_ref[...], high, nt, preferred_element_type=F32)
            two = lax.dot_general(second_ref[0:64, :], low, nt, preferred_element_type=F32)
            both = one[0:64] + one[64:128] + two
            for k in range(2):
                zs[step, :, u * 2 + k] = both[:, k * 128:(k + 1) * 128].reshape(8, 8, 128)

    source = lat * 4 + yy
    my_g, my_s = source // 8, lax.rem(source, 8)

    to_x = [lax.rem(xx + 2 * dx, 4) // 2 * 2 + core for dx in range(2)]
    to_lats = {(dz, dx): lax.rem(zz + dz, 4) * 4 + to_x[dx] for dz in range(4) for dx in range(2)}
    to_l8 = {key: value // 2 for key, value in to_lats.items()}
    crossed = jnp.where(core == 1, other, lev)

    def send_in(step):
        to_lev = crossed if step else lev

        @pl.loop(0, 8)
        def _(k):
            to_lon = lax.rem(lon + k, 8)
            for dz in (2, 1, 3, 0):
                for dx in range(2):
                    to_lat = to_lats[dz, dx]
                    src = zs.at[step, to_lon, to_l8[dz, dx]]
                    dst = zr.at[step, my_g, my_s]

                    def remote():
                        pltpu.make_async_remote_copy(
                            src_ref=src, dst_ref=dst,
                            send_sem=in_send.at[step], recv_sem=in_recv.at[step],
                            device_id=(to_lon, to_lat, to_lev), device_id_type=MESH,
                        ).start()

                    if dz or dx:
                        remote()
                        continue
                    mine = jnp.logical_and(
                        jnp.logical_and(k == 0, to_lat == lat), to_lev == lev
                    )

                    @pl.when(jnp.logical_not(mine))
                    def _():
                        remote()

                    @pl.when(mine)
                    def _():
                        pltpu.make_async_copy(src, dst, in_recv.at[step]).start()

    def wait_in_sends(step):
        flip = jnp.logical_and(core == 1, step >= 1)
        has_self = jnp.logical_and(half == core, jnp.logical_not(flip))

        @pl.when(has_self)
        def _():
            wait_bytes(zs.at[step, pl.ds(0, 7)], in_send.at[step])
            wait_bytes(zs.at[step, 0, pl.ds(0, 7)], in_send.at[step])

        @pl.when(jnp.logical_not(has_self))
        def _():
            wait_bytes(zs.at[step], in_send.at[step])

    def send_round_two():
        for off in range(1, 16):
            pl.semaphore_signal(
                round_two, inc=1, device_id=(lon, lax.rem(lat + off, 16), lev), device_id_type=MESH
            )

    loads[0].wait()
    loads[5].wait()
    make_products(0, lambda r: fields[0, r, :] * fields[5, r, :])
    loads[1].wait()
    loads[3].wait()
    make_products(3, lambda r: fields[1, r, :] * fields[3, r, :])
    pl.semaphore_wait(barrier, 31)
    for copy in halo_copies:
        copy.start()
    send_lon(0, 0)
    send_lon(0, 1)
    send_round_two()
    wait_bytes(quarter, pc_recv.at[1])
    push(rows_of(zz, xx), away_id, pz_recv.at[0], 0)
    push(rows_of(zz, xx), beyond_id, pz_recv.at[1], 0)
    spread_x(0, zz)
    make_products(1, lambda r: fields[0, r, :] * fields[1, r, :])
    loads[4].wait()
    make_products(2, lambda r: fields[0, r, :] * fields[4, r, :])
    sign = jnp.where(lev == 0, F32(-0.5), F32(0.5))
    halo_copies[0].wait_recv()
    make_products(4, lambda r: halo[0, r, :] * (fields[0, r, :] * sign))
    wait_bytes(quarter, pz_recv.at[1])
    push(rows_of(toward, xx), away_id, pz_recv.at[2], 0)
    spread_x(2, toward)
    wait_bytes(quarter, pz_recv.at[0])
    spread_x(1, away)
    relay_x(0, blocks[0])
    wait_lon_sends(0)
    send_lon(1, 0)
    send_lon(1, 1)
    zonal(0)
    pl.semaphore_wait(round_two, 15)
    send_in(0)
    halo_copies[1].wait_recv()
    make_products(
        5,
        lambda r: halo[0, r, :] * (fields[3, r, :] * sign)
        - 0.25 * (fields[4, r, :] - 2.0 * halo[1, r, :]),
    )
    wait_lon_sends(1)
    send_lon(2, 0)
    send_lon(2, 1)
    wait_bytes(quarter, pz_recv.at[2])
    spread_x(3, far)
    relay_x(2, blocks[2])
    relay_x(1, blocks[1])
    zonal(1)
    send_in(1)
    relay_x(3, blocks[3])
    zonal(2)
    send_in(2)

    for slot in range(4):
        for side in range(2):
            wait_bytes(pbuf.at[0, :, pl.ds(0, 32)], px_recv.at[slot, 2 + side])
    to_sibling = pltpu.make_async_remote_copy(
        src_ref=pbuf.at[core], dst_ref=pbuf.at[core],
        send_sem=p_send.at[2], recv_sem=pc_recv.at[0],
        device_id=(lon + 1 - 2 * core, lat, lev), device_id_type=MESH,
    )
    to_sibling.start()

    def prepare(which):
        @pl.loop(0, 8)
        def _(g):
          for u in range(8):
            for col in range(4):
                pieces = [
                    pbuf[which, col, pl.ds(g * 128 + u * 2 + k, 8, stride=16), :]
                    for k in range(2)
                ]
                high, low = split(jnp.concatenate(pieces, axis=0))
                rows = pl.ds(pl.multiple_of(g * 128 + u * 16, 16), 16)
                p_hi[which, rows, col * 128:(col + 1) * 128] = high
                p_lo[which, rows, col * 128:(col + 1) * 128] = low

    lane = lax.broadcasted_iota(jnp.int32, (64, 128), 1)
    low_lanes = lax.broadcasted_iota(jnp.int32, (32, 128), 1) < 64

    def transpose_in(step):
        wait_bytes(zr.at[step], in_recv.at[step])
        v = [zr[step, :, s].reshape(64, 128) for s in range(8)]
        for k in range(3):
            bit = 1 << k
            low_half = (lane & bit) == 0
            new = list(v)
            for a in range(8):
                if a & bit:
                    continue
                b = a | bit
                new[a] = jnp.where(low_half, v[a], pltpu.roll(v[b], bit, 1))
                new[b] = jnp.where(low_half, pltpu.roll(v[a], 128 - bit, 1), v[b])
            v = new
        for j in range(8):
            for g in range(8):
                zct[g, pl.ds(j, 8, stride=8), :] = v[j][g * 8:(g + 1) * 8]
        high, low = split(jnp.concatenate([zct[g] for g in range(8)], axis=1))
        zb[0:64, :] = high
        zb[64:128, :] = low

    def project(step, which):
        for col in range(2):
            cols = slice(col * 256, (col + 1) * 256)
            one = jnp.dot(zb[...], p_hi[which, :, cols], preferred_element_type=F32)
            two = jnp.dot(zb[0:64, :], p_lo[which, :, cols], preferred_element_type=F32)
            both = one[0:64] + one[64:128] + two
            for k in range(2):
                t = which * 4 + col * 2 + k
                a = both[0:32, k * 128:(k + 1) * 128]
                b = both[32:64, k * 128:(k + 1) * 128]
                even = jnp.where(low_lanes, a, pltpu.roll(b, 64, 1))
                odd = jnp.where(low_lanes, pltpu.roll(a, 64, 1), b)
                outs[step, 2 * t] = even.reshape(4, 8, 128)
                outs[step, 2 * t + 1] = odd.reshape(4, 8, 128)

        for j in range(8):
            to_lat = which * 8 + lax.rem(lat + 4 + j, 8)

            @pl.when(to_lat != lat)
            def _():
                pltpu.make_async_remote_copy(
                    src_ref=outs.at[step, to_lat], dst_ref=gath.at[step, half, :, l8],
                    send_sem=out_send.at[step], recv_sem=out_recv.at[step],
                    device_id=(lon, to_lat, lev), device_id_type=MESH,
                ).start()

            @pl.when(to_lat == lat)
            def _():
                pltpu.make_async_copy(
                    outs.at[step, to_lat], gath.at[step, half, :, l8], out_recv.at[step]
                ).start()

    prepare(core)
    transpose_in(0)
    project(0, core)
    wait_bytes(pbuf.at[0], pc_recv.at[0])
    prepare(1 - core)
    project(0, 1 - core)
    transpose_in(1)
    project(1, core)
    project(1, 1 - core)
    transpose_in(2)
    project(2, core)
    project(2, 1 - core)

    def assemble(step):
        wait_bytes(gath.at[step], out_recv.at[step])
        for h2 in range(2):
            field = 3 * h2 + step
            for t in range(2):
                block = gath[step, h2, 2 * t:2 * t + 2].reshape(128, 128)
                turned = block.T
                for h in range(2):
                    sb = 2 * h + t
                    for n0 in range(0, 64, 8):
                        out_ref[pl.ds((n0 * 6 + field) * 4 + sb, 8, stride=24), :] = (
                            turned[h * 64 + n0:h * 64 + n0 + 8]
                        )

    for step in range(STEPS):
        assemble(step)

    wait_lon_sends(2)
    for copy in halo_copies:
        copy.wait_send()
    for step in range(STEPS):
        wait_in_sends(step)
        wait_bytes(outs.at[step, pl.ds(0, 15)], out_send.at[step])
    wait_bytes(pbuf.at[0, :, pl.ds(0, 192)], p_send.at[0])
    wait_bytes(pbuf.at[0, :, pl.ds(0, 512)], p_send.at[1])
    wait_bytes(pbuf.at[0, :, pl.ds(0, 256)], p_send.at[3])
    to_sibling.wait_send()


def on_device(fields_grid, hermite_proj):
    first_cat, twiddle, second_cat = tables()
    vmem = pl.BlockSpec(memory_space=pltpu.VMEM)
    dma = pltpu.SemaphoreType.DMA
    out = pl.pallas_call(
        kernel,
        out_shape=jax.ShapeDtypeStruct((1536, 128), F32),
        in_specs=[pl.BlockSpec(memory_space=pltpu.HBM)] * 5,
        out_specs=vmem,
        scratch_shapes=[
            pltpu.VMEM((6, 64, 1024), F32),
            pltpu.VMEM((128, 192), BF16),
            pltpu.VMEM((128, 128), F32),
            pltpu.VMEM((128, 256), BF16),
            pltpu.VMEM((2, 64, 1024), F32),
            pltpu.VMEM((6 * 512, 128), F32),
            pltpu.VMEM((3, 8, 128, 128), F32),
            pltpu.VMEM((8, 128, 256), BF16),
            pltpu.VMEM((8, 128, 256), BF16),
            pltpu.VMEM((3, 8, 8, 8, 128), F32),
            pltpu.VMEM((3, 8, 8, 8, 128), F32),
            pltpu.VMEM((8, 64, 128), F32),
            pltpu.VMEM((2, 4, 1024, 128), F32),
            pltpu.VMEM((2, 1024, 512), BF16),
            pltpu.VMEM((2, 1024, 512), BF16),
            pltpu.VMEM((128, 1024), BF16),
            pltpu.VMEM((3, 16, 4, 8, 128), F32),
            pltpu.VMEM((3, 2, 4, 8, 8, 128), F32),
            dma((2,)), dma((2,)), dma((3,)), dma((3,)), dma((3,)), dma((3,)), dma((3,)), dma((3,)),
            dma((4,)), dma((3,)), dma((4, 4)), dma((2,)), dma((9,)),
            pltpu.SemaphoreType.REGULAR,
        ],
        compiler_params=pltpu.CompilerParams(
            collective_id=0, has_side_effects=True, vmem_limit_bytes=60 * 1024 * 1024
        ),
    )(fields_grid, hermite_proj, first_cat, twiddle, second_cat)
    return out.reshape(64, 6, 1, 512)


def solution(mesh):
    in_specs = (P(None, "lev", "lat", "lon"), P("lat", None))
    out_specs = P("lat", None, "lev", "lon")
    return jax.shard_map(
        on_device, mesh=mesh, in_specs=in_specs, out_specs=out_specs, check_vma=False
    )
```

time: 89 us -> 69.2 us (0.78)
  Pallas kernels: 82.9 us -> 66.5 us
  local copies, waits for them, and re-layouts: 5.76 us -> 2.55 us
    pallas_call x1, Pallas kernels: 82.9 us -> 66.5 us  [on_device(): pl.pallas_call(kernel, out_shape=jax.ShapeDtypeStruct((1536, 128), F32),...]
    unnamed x11 -> x1, local copies, waits for them, and re-layouts: 5.76 us -> 2.55 us
where the time goes in v1:
time: 69.2 us; the launch traced here: 69.1 us
  Pallas kernels  66.5 us (96%)
  local copies, waits for them, and re-layouts  2.55 us (4%)
    pallas_call x1, Pallas kernels, on_device(): pl.pallas_call(kernel, out_shape=jax.ShapeDtypeStruct((1536, 128), F32),...  66.5 us
    unnamed x1, local copies, waits for them, and re-layouts  2.55 us

profile of v1, /device:TPU:1, one launch (start us, length us, event | category | flops | bytes accessed | tf_op | source)
XLA Modules:
  0.0 69.1 jit_solution(17116962650567319678)
XLA Ops:
  0.0 66.5 %shard_map.55 = f32[1536,128]{1,0:T(8,128)} custom-call(f32[6,1,64,1024]{3,2,1,0:T(8,128)} %fields_hbm.1, f32[64,1024]{1,0:T(8,128)} %herm_hbm.1, bf16[128,192]{1,0:T(8,128)(2,1)} %constant.6.clone.first_hbm, f32[128,128]{1,0:T(8,128)} %constant.7.clone.twiddle_hbm, bf16[128,256]{1,0:T(8,128)(2,1)} %constant.8.clone.second_hbm), custom_call_target="tpu_custom_call" | custom-call | tf_op jit(solution)/shard_map/pallas_call | solution.py:458
  66.5 2.6 %copy.9 = f32[64,6,1,512]{3,2,1,0:T(1,128)} copy(f32[64,6,1,512]{3,2,1,0:T(1,128)} %bitcast.1) | data formatting | bytes 1572864

commit v2 on v1

--- a/solution.py
+++ b/solution.py
@@ -54,8 +54,8 @@
 
 
 def kernel(
-    fields_hbm, herm_hbm, first_hbm, twiddle_hbm, second_hbm, out_ref,
-    fields, first_ref, twiddle_ref, second_ref, halo, xs, xr, b_hi, b_lo, zs, zr, zct, pbuf, p_hi, p_lo, zb, outs, gath,
+    fields_hbm, herm_hbm, first_hbm, twiddle_hbm, second_hbm, gath,
+    fields, first_ref, twiddle_ref, second_ref, halo, xs, xr, b_hi, b_lo, zs, zr, zct, pbuf, p_hi, p_lo, zb, outs,
     halo_send, halo_recv, lon_send, lon_recv, in_send, in_recv, out_send, out_recv,
     p_send, pz_recv, px_recv, pc_recv, load, round_two,
 ):
@@ -66,22 +66,6 @@
     zz, xx = lat // 4, lax.rem(lat, 4)
     half, l8 = lax.rem(lat, 2), lat // 2
     other = 1 - lev
-
-    away = lax.rem(zz + 3 + 2 * lev, 4)
-    partner_id = (lon, lat, other)
-    away_id = (lon, away * 4 + xx, other)
-    barrier = pltpu.get_barrier_semaphore()
-
-    def greet(device_id):
-        pl.semaphore_signal(barrier, inc=1, device_id=device_id, device_id_type=MESH)
-
-    for off in range(1, 16):
-        greet((lon, lax.rem(lat + off, 16), lev))
-    greet(away_id)
-    for off in range(1, 8):
-        greet((lax.rem(lon + off, 8), lat, lev))
-    for off in range(8):
-        greet((lax.rem(lon + off, 8), lat, other))
 
     loads = [
         pltpu.make_async_copy(fields_hbm.at[f, 0], fields.at[f], load.at[f]) for f in (0, 5, 1, 3, 4)
@@ -101,6 +85,22 @@
     ]
     for copy in constants:
         copy.start()
+
+    away = lax.rem(zz + 3 + 2 * lev, 4)
+    partner_id = (lon, lat, other)
+    away_id = (lon, away * 4 + xx, other)
+    barrier = pltpu.get_barrier_semaphore()
+
+    def greet(device_id):
+        pl.semaphore_signal(barrier, inc=1, device_id=device_id, device_id_type=MESH)
+
+    for off in range(1, 16):
+        greet((lon, lax.rem(lat + off, 16), lev))
+    greet(away_id)
+    for off in range(1, 8):
+        greet((lax.rem(lon + off, 8), lat, lev))
+    for off in range(8):
+        greet((lax.rem(lon + off, 8), lat, other))
 
     halo_copies = []
     for slot, field in enumerate((2, 4)):
@@ -296,20 +296,19 @@
     loads[4].wait()
     make_products(2, lambda r: fields[0, r, :] * fields[4, r, :])
     sign = jnp.where(lev == 0, F32(-0.5), F32(0.5))
-    halo_copies[0].wait_recv()
-    make_products(4, lambda r: halo[0, r, :] * (fields[0, r, :] * sign))
+    send_lon(1, 0)
     wait_bytes(quarter, pz_recv.at[1])
     push(rows_of(toward, xx), away_id, pz_recv.at[2], 0)
     spread_x(2, toward)
     wait_bytes(quarter, pz_recv.at[0])
     spread_x(1, away)
-    relay_x(0, blocks[0])
-    wait_lon_sends(0)
-    send_lon(1, 0)
+    halo_copies[0].wait_recv()
+    make_products(4, lambda r: halo[0, r, :] * (fields[0, r, :] * sign))
     send_lon(1, 1)
     zonal(0)
     pl.semaphore_wait(round_two, 15)
     send_in(0)
+    relay_x(0, blocks[0])
     halo_copies[1].wait_recv()
     make_products(
         5,
@@ -422,24 +421,11 @@
     project(2, core)
     project(2, 1 - core)
 
-    def assemble(step):
+    for step in range(STEPS):
         wait_bytes(gath.at[step], out_recv.at[step])
-        for h2 in range(2):
-            field = 3 * h2 + step
-            for t in range(2):
-                block = gath[step, h2, 2 * t:2 * t + 2].reshape(128, 128)
-                turned = block.T
-                for h in range(2):
-                    sb = 2 * h + t
-                    for n0 in range(0, 64, 8):
-                        out_ref[pl.ds((n0 * 6 + field) * 4 + sb, 8, stride=24), :] = (
-                            turned[h * 64 + n0:h * 64 + n0 + 8]
-                        )
-
-    for step in range(STEPS):
-        assemble(step)
 
     wait_lon_sends(2)
+    wait_lon_sends(0)
     for copy in halo_copies:
         copy.wait_send()
     for step in range(STEPS):
@@ -451,15 +437,35 @@
     to_sibling.wait_send()
 
 
+def assemble(gath_hbm, out_ref, gath, load):
+    copies = [
+        pltpu.make_async_copy(gath_hbm.at[step], gath.at[step], load.at[step]) for step in range(STEPS)
+    ]
+    for copy in copies:
+        copy.start()
+    for step in range(STEPS):
+        copies[step].wait()
+        for half in range(2):
+            field = 3 * half + step
+            for t in range(2):
+                turned = gath[step, half, 2 * t:2 * t + 2].reshape(128, 128).T
+                for h in range(2):
+                    sb = 2 * h + t
+                    for n0 in range(0, 64, 8):
+                        out_ref[pl.ds((n0 * 6 + field) * 4 + sb, 8, stride=24), :] = (
+                            turned[h * 64 + n0:h * 64 + n0 + 8]
+                        )
+
+
 def on_device(fields_grid, hermite_proj):
     first_cat, twiddle, second_cat = tables()
-    vmem = pl.BlockSpec(memory_space=pltpu.VMEM)
+    hbm = pl.BlockSpec(memory_space=pltpu.HBM)
     dma = pltpu.SemaphoreType.DMA
-    out = pl.pallas_call(
+    gathered = pl.pallas_call(
         kernel,
-        out_shape=jax.ShapeDtypeStruct((1536, 128), F32),
-        in_specs=[pl.BlockSpec(memory_space=pltpu.HBM)] * 5,
-        out_specs=vmem,
+        out_shape=jax.ShapeDtypeStruct((3, 2, 4, 8, 8, 128), F32),
+        in_specs=[hbm] * 5,
+        out_specs=hbm,
         scratch_shapes=[
             pltpu.VMEM((6, 64, 1024), F32),
             pltpu.VMEM((128, 192), BF16),
@@ -478,7 +484,6 @@
             pltpu.VMEM((2, 1024, 512), BF16),
             pltpu.VMEM((128, 1024), BF16),
             pltpu.VMEM((3, 16, 4, 8, 128), F32),
-            pltpu.VMEM((3, 2, 4, 8, 8, 128), F32),
             dma((2,)), dma((2,)), dma((3,)), dma((3,)), dma((3,)), dma((3,)), dma((3,)), dma((3,)),
             dma((4,)), dma((3,)), dma((4, 4)), dma((2,)), dma((9,)),
             pltpu.SemaphoreType.REGULAR,
@@ -487,6 +492,14 @@
             collective_id=0, has_side_effects=True, vmem_limit_bytes=60 * 1024 * 1024
         ),
     )(fields_grid, hermite_proj, first_cat, twiddle, second_cat)
+    out = pl.pallas_call(
+        assemble,
+        out_shape=jax.ShapeDtypeStruct((1536, 128), F32),
+        in_specs=[hbm],
+        out_specs=pl.BlockSpec(memory_space=pltpu.VMEM),
+        scratch_shapes=[pltpu.VMEM((3, 2, 4, 8, 8, 128), F32), dma((3,))],
+        compiler_params=pltpu.CompilerParams(vmem_limit_bytes=60 * 1024 * 1024),
+    )(gathered)
     return out.reshape(64, 6, 1, 512)
 
 

time: 69.2 us -> 68.1 us (0.984)
  local copies, waits for them, and re-layouts: 2.55 us -> 0 us
  Pallas kernels: 66.5 us -> 68 us
    unnamed x1 -> x0, local copies, waits for them, and re-layouts: 2.55 us -> none
    pallas_call x1 -> x2, Pallas kernels: 66.5 us -> 68 us  [the longest x1 65.7 us: on_device(): pl.pallas_call(kernel, out_shape=jax.ShapeDtypeStruct((3, 2, 4, 8, 8, 128...]
where the time goes in v2:
time: 68.1 us; the launch traced here: 68 us
  Pallas kernels  68 us (100%)
    pallas_call x1, Pallas kernels, on_device(): pl.pallas_call(kernel, out_shape=jax.ShapeDtypeStruct((3, 2, 4, 8, 8, 128...  65.7 us
    pallas_call x1, Pallas kernels, on_device(): pl.pallas_call(assemble, out_shape=jax.ShapeDtypeStruct((1536, 128), F32)...  2.26 us

profile of v2, /device:TPU:1, one launch (start us, length us, event | category | flops | bytes accessed | tf_op | source)
XLA Modules:
  0.0 68.0 jit_solution(6863456915866482790)
XLA Ops:
  0.0 65.7 %shard_map.55.gath_hbm = f32[3,2,4,8,8,128]{5,4,3,2,1,0:T(8,128)} custom-call(f32[6,1,64,1024]{3,2,1,0:T(8,128)} %fields_hbm.1, f32[64,1024]{1,0:T(8,128)} %herm_hbm.1, bf16[128,192]{1,0:T(8,128)(2,1)} %constant.6.clone.first_hbm, f32[128,128]{1,0:T(8,128)} %constant.7.clone.twiddle_hbm, bf16[128,256]{1,0:T(8,128)(2,1)} %constant.8.clone.second_hbm), custom_call_target="tpu_custom_call" | custom-call | tf_op jit(solution)/shard_map/pallas_call | solution.py:464
  65.7 2.3 %shard_map.56 = f32[1536,128]{1,0:T(8,128)} custom-call(f32[3,2,4,8,8,128]{5,4,3,2,1,0:T(8,128)} %shard_map.55.gath_hbm), custom_call_target="tpu_custom_call" | custom-call | tf_op jit(solution)/shard_map/pallas_call | solution.py:495

commit v3 on v2

--- a/solution.py
+++ b/solution.py
@@ -392,7 +392,7 @@
                 outs[step, 2 * t + 1] = odd.reshape(4, 8, 128)
 
         for j in range(8):
-            to_lat = which * 8 + lax.rem(lat + 4 + j, 8)
+            to_lat = which * 8 + lax.rem(lat + 2 + j, 8)
 
             @pl.when(to_lat != lat)
             def _():

time: 68.1 us -> 67.2 us (0.987)
  Pallas kernels: 68 us -> 66.9 us
    pallas_call x1, Pallas kernels: 65.7 us -> 64.6 us  [on_device(): pl.pallas_call(kernel, out_shape=jax.ShapeDtypeStruct((3, 2, 4, 8, 8, 128...]
where the time goes in v3:
time: 67.2 us; the launch traced here: 66.9 us
  Pallas kernels  66.9 us (100%)
    pallas_call x1, Pallas kernels, on_device(): pl.pallas_call(kernel, out_shape=jax.ShapeDtypeStruct((3, 2, 4, 8, 8, 128...  64.6 us
    pallas_call x1, Pallas kernels, on_device(): pl.pallas_call(assemble, out_shape=jax.ShapeDtypeStruct((1536, 128), F32)...  2.26 us

profile of v3, /device:TPU:1, one launch (start us, length us, event | category | flops | bytes accessed | tf_op | source)
XLA Modules:
  0.0 66.9 jit_solution(15431766761002039348)
XLA Ops:
  0.0 64.6 %shard_map.55.gath_hbm = f32[3,2,4,8,8,128]{5,4,3,2,1,0:T(8,128)} custom-call(f32[6,1,64,1024]{3,2,1,0:T(8,128)} %fields_hbm.1, f32[64,1024]{1,0:T(8,128)} %herm_hbm.1, bf16[128,192]{1,0:T(8,128)(2,1)} %constant.6.clone.first_hbm, f32[128,128]{1,0:T(8,128)} %constant.7.clone.twiddle_hbm, bf16[128,256]{1,0:T(8,128)(2,1)} %constant.8.clone.second_hbm), custom_call_target="tpu_custom_call" | custom-call | tf_op jit(solution)/shard_map/pallas_call | solution.py:464
  64.7 2.3 %shard_map.56 = f32[1536,128]{1,0:T(8,128)} custom-call(f32[3,2,4,8,8,128]{5,4,3,2,1,0:T(8,128)} %shard_map.55.gath_hbm), custom_call_target="tpu_custom_call" | custom-call | tf_op jit(solution)/shard_map/pallas_call | solution.py:495
